TPU v7x, 32 devices: a whole 2x2x4 slice. The times are simulated.
32 devices in a mesh: slab: 4 (over y, x), energy: 8 (over z, core).
Axes of the slice: x: 2, y: 2, z: 4, core: 2. Of those that a mesh axis runs over, the one named last changes fastest.
Arguments:
- energies: float32 [8], P('energy'), may hold values from -1 to 1
- broadening: float32 [8], P('energy'), may hold values from 0.3 to 1
- hamiltonian: float32 [1024, 256], P('slab'), as said below
- coupling: float32 [1024, 256], P('slab'), may hold values from -0.21875 to 0.21875
- propagator: float32 [2, 6, 8, 8], replicated, may hold values from -2 to 2
- neighbors: int32 [1024, 32], P('slab'), may hold values from 0 to 255, as said below
- phonon_modes: int32 [1024, 32], P('slab'), may hold values from 0 to 5
Outputs:
- green_blocks: float32 [8, 2, 1024, 256], P('energy', None, 'slab')
- self_energy: float32 [8, 2, 32768], P('energy', None, 'slab')
Inputs may be any that keep to these rules, and one draw needn't show every extreme that they name: `hamiltonian`: each block of 256 rows is symmetric. `neighbors`: an orbital is never its own neighbour.
All inputs are finite; a program needn't handle non-finite values.
Results may differ from a plain program's by a relative error of at most 0.0001.
Values sent between devices are 32-bit elements; how exact they have to be, the bound alone decides.
A program may use at most 128 MiB of HBM per device.

v0:
```python
import math

import jax
import jax.numpy as jnp
from jax import lax
from jax.sharding import PartitionSpec as P

B = 256
NEIGH = 32


HIGHEST = lax.Precision.HIGHEST


def shifted_2(block, axis, distance):
    devices = range(lax.axis_size(axis))
    route = [(i - distance, i) for i in devices if i - distance in devices]
    return lax.ppermute(block, axis, route)


def complex_product(left, right):
    left_real, left_imag = (left[:, 0], left[:, 1])
    right_real, right_imag = (right[:, 0], right[:, 1])
    first = jnp.matmul(left_real, right_real, precision=HIGHEST)
    second = jnp.matmul(left_imag, right_imag, precision=HIGHEST)
    mixed = jnp.matmul(left_real + left_imag, right_real + right_imag, precision=HIGHEST)
    return jnp.stack([first - second, mixed - first - second], axis=1)


def newton_step(schur, inverse):
    identity = jnp.eye(schur.shape[-1], dtype=jnp.float32)
    residue = -complex_product(schur, inverse)
    residue = residue.at[:, 0].add(2.0 * identity)
    return complex_product(inverse, residue)


def jacobi_refine(schur):
    identity = jnp.eye(schur.shape[-1], dtype=jnp.float32)
    diagonal = jnp.diagonal(schur, axis1=2, axis2=3)
    diag_real, diag_imag = (diagonal[:, 0], diagonal[:, 1])
    modulus = diag_real * diag_real + diag_imag * diag_imag
    inv_real = diag_real / modulus
    inv_imag = -diag_imag / modulus
    outer_real = (
        inv_real[:, :, None] * inv_real[:, None, :] - inv_imag[:, :, None] * inv_imag[:, None, :]
    )
    outer_imag = (
        inv_real[:, :, None] * inv_imag[:, None, :] + inv_imag[:, :, None] * inv_real[:, None, :]
    )
    schur_real, schur_imag = (schur[:, 0], schur[:, 1])
    first_real = 2.0 * identity * inv_real[:, :, None] - (
        outer_real * schur_real - outer_imag * schur_imag
    )
    first_imag = 2.0 * identity * inv_imag[:, :, None] - (
        outer_real * schur_imag + outer_imag * schur_real
    )
    first_iterate = jnp.stack([first_real, first_imag], axis=1)
    return newton_step(schur, first_iterate)


def convolve_modes(kernel, values, one_hot):
    spread = one_hot[:, None, None, :] * values[None]
    real_part = jnp.einsum(
        "mef,mfp->ep", kernel[0], spread[:, :, 0], precision=HIGHEST
    ) - jnp.einsum("mef,mfp->ep", kernel[1], spread[:, :, 1], precision=HIGHEST)
    imag_part = jnp.einsum(
        "mef,mfp->ep", kernel[0], spread[:, :, 1], precision=HIGHEST
    ) + jnp.einsum("mef,mfp->ep", kernel[1], spread[:, :, 0], precision=HIGHEST)
    return jnp.stack([real_part, imag_part], axis=1)


def body(energies, broadening, hamiltonian, coupling, propagator, neighbors, phonon_modes):
    coupling_scale = 2.0 * math.sqrt(B / NEIGH)
    e_dev = energies.shape[0]
    orbitals = hamiltonian.shape[0]
    listed = neighbors.shape[1]
    mode_count = propagator.shape[1]
    identity = jnp.eye(orbitals, dtype=jnp.float32)
    shifted = jnp.stack(
        [
            energies[:, None, None] * identity - hamiltonian[None],
            broadening[:, None, None] * identity,
        ],
        axis=1,
    )

    def advance(operand):
        through = jnp.matmul(
            jnp.matmul(coupling, operand[0], precision=HIGHEST), coupling.T, precision=HIGHEST
        )
        schur_new = shifted - through
        return (schur_new, jacobi_refine(schur_new))

    def remain(operand):
        return (operand[1], operand[2])

    slab_count = lax.axis_size("slab")
    slab_index = lax.axis_index("slab")
    incoming = jnp.zeros((e_dev, 2, orbitals, orbitals), jnp.float32)
    schur = jnp.zeros_like(incoming)
    inverse = jnp.zeros_like(incoming)
    for step_index in range(slab_count):
        schur, inverse = lax.cond(
            slab_index == step_index, advance, remain, (incoming, schur, inverse)
        )
        if step_index + 1 < slab_count:
            incoming = shifted_2(inverse, "slab", 1)
    early_product = complex_product(schur, inverse)
    pair_mask = (
        neighbors[:, :, None] == jnp.arange(orbitals, dtype=jnp.int32)[None, None, :]
    ).astype(jnp.float32)
    pair_green = jnp.einsum("ecij,ikj->ecik", inverse, pair_mask, precision=HIGHEST).reshape(
        e_dev, 2, orbitals * listed
    )
    modes_flat = phonon_modes.reshape(-1)
    mode_ids = jnp.arange(mode_count, dtype=jnp.int32)
    one_hot = (modes_flat[None, :] == mode_ids[:, None]).astype(jnp.float32)
    first_energy = lax.axis_index("energy") * e_dev
    kernel = lax.dynamic_slice(
        propagator, (0, 0, 0, first_energy), (2, mode_count, e_dev * lax.axis_size("energy"), e_dev)
    )
    total = lax.psum_scatter(
        convolve_modes(kernel, pair_green, one_hot), "energy", scatter_dimension=0, tiled=True
    )
    self_part = coupling_scale * total
    reshaped = self_part.reshape(e_dev, 2, orbitals, listed)
    self_dense = jnp.einsum("ecik,ikj->ecij", reshaped, pair_mask, precision=HIGHEST)
    residue = complex_product(self_dense, inverse) - early_product
    residue = residue.at[:, 0].add(2.0 * identity)
    green_block = complex_product(inverse, residue)
    return (green_block, self_part)


def solution(mesh):
    return jax.shard_map(
        body,
        mesh=mesh,
        in_specs=(
            P("energy"),
            P("energy"),
            P("slab", None),
            P("slab", None),
            P(),
            P("slab", None),
            P("slab", None),
        ),
        out_specs=(P("energy", None, "slab", None), P("energy", None, "slab")),
        check_vma=False,
    )
```

profile of v0, /device:TPU:5, one launch (start us, length us, event | category | flops | bytes accessed | tf_op | source)
XLA Modules:
  0.0 260.8 jit_solution(4348681585417524408)
XLA Ops:
  7.2 0.0 all-reduce.3.cloned.1.call-start
  8.5 1.0 subtract_bitcast_fusion.10
  9.6 0.9 conditional.4
  9.6 0.8 broadcast.3799
  10.5 0.0 copy-start.2
  10.5 3.1 %collective-permute-start = (f32[1,2,256,256]{3,2,1,0:T(8,128)S(1)}, f32[1,2,256,256]{3,2,1,0:T(8,128)S(1)}, u32[]{:S(2)}, u32[]{:S(2)}) collective-permute-start(f32[1,2,256,256]{3,2,1,0:T(8,128)S(1)} %get-tuple-element.149), channel_id=1, source_target_pairs={{0,8},{8,16},{16,24},{1,9},{9,17},{17,25},{2,10},{10,18},{18,26},{... | collective-permute-start | bytes 1572872 | tf_op jit(solution)/shard_map/ppermute | solution.py:18
  13.6 12.5 %collective-permute-done = f32[1,2,256,256]{3,2,1,0:T(8,128)S(1)} collective-permute-done((f32[1,2,256,256]{3,2,1,0:T(8,128)S(1)}, f32[1,2,256,256]{3,2,1,0:T(8,128)S(1)}, u32[]{:S(2)}, u32[]{:S(2)}) %collective-permute-start) | collective-permute-done | bytes 524320 | tf_op jit(solution)/shard_map/ppermute | solution.py:18
  26.1 2.4 collective-permute-start.1
  28.4 0.1 copy.38
  28.5 0.1 eq.338
  28.6 70.5 %collective-permute-done.1 = f32[1,2,256,256]{3,2,1,0:T(8,128)S(1)} collective-permute-done((f32[1,2,256,256]{3,2,1,0:T(8,128)S(1)}, f32[1,2,256,256]{3,2,1,0:T(8,128)S(1)}, u32[]{:S(2)}, u32[]{:S(2)}) %collective-permute-start.1) | collective-permute-done | bytes 524320 | tf_op jit(solution)/shard_map/ppermute | solution.py:18
  99.2 30.5 %conditional.6 = ((f32[1,2,256,256]{3,2,1,0:T(8,128)}, f32[1,2,256,256]{3,2,1,0:T(8,128)S(1)})) conditional(s32[]{:T(128)} %convert_element_type.32, (f32[1,2,256,256]{3,2,1,0:T(8,128)}, f32[1,2,256,256]{3,2,1,0:T(8,128)S(1)}) %get-tuple-element.236, (f32[1,2,256,256]{3,2,1,0:T(8,128)S(1)}, f32[256,256]{1,0:T(8,128)}, ...), branch_computations={%region_4.5_spmd, %region_5.0_spmd} | conditional | flops 2016022016 | bytes 15752216 | solution.py:103
  99.2 1.6 convolution_bitcast_fusion.5
  100.7 2.4 fusion.101
  103.1 17.2 %copy.34 = f32[2,256,256]{0,2,1:T(8,128)} copy(f32[2,256,256]{2,1,0:T(8,128)} %bitcast.58) | data formatting | bytes 1048576 | tf_op jit(solution)/shard_map/cond/branch_1_fun/sub | solution.py:91
  120.3 2.3 gather_fusion.2
  122.6 0.3 divide_reduce_fusion.5
  123.0 1.2 fusion.107
  124.2 1.3 fusion.121
  125.5 1.3 fusion.118
  126.9 1.4 fusion.105
  128.4 0.4 fusion.112
  128.8 0.4 fusion.110
  129.2 0.4 fusion.103
  129.7 1.9 collective-permute-start.2
  131.7 0.1 copy.36
  131.8 0.0 copy-done.1
  131.8 0.1 constant_dynamic-slice_fusion.1
  131.9 0.1 copy.50
  132.0 0.1 copy.51
  132.1 0.7 dynamic-slice.36
  132.8 12.0 %collective-permute-done.2 = f32[1,2,256,256]{3,2,1,0:T(8,128)S(1)} collective-permute-done((f32[1,2,256,256]{3,2,1,0:T(8,128)S(1)}, f32[1,2,256,256]{3,2,1,0:T(8,128)S(1)}, u32[]{:S(2)}, u32[]{:S(2)}) %collective-permute-start.2) | collective-permute-done | bytes 524320 | tf_op jit(solution)/shard_map/ppermute | solution.py:18
  144.7 2.8 %conditional.7 = (f32[1,2,256,256]{3,2,1,0:T(8,128)}, f32[1,1,256,256]{3,2,1,0:T(8,128)}, f32[1,1,256,256]{3,2,1,0:T(8,128)}, f32[256,256]{1,0:T(8,128)S(1)}, f3...) conditional(s32[]{:T(128)} %convert_element_type.31, (f32[1,2,256,256]{3,2,1,0:T(8,128)S(1)}, ...), branch_computations={%region_6.7_spmd, %region_7.8_spmd} | conditional | flops 2016022016 | bytes 16538672 | solution.py:103
  144.7 0.9 fusion.272
  145.6 0.9 copy.100
  146.5 0.9 copy.99
  147.5 4.6 %fusion.207 = f32[1,2,256,32]{3,1,2,0:T(2,128)S(1)} fusion(s32[256,32]{1,0:T(8,128)S(1)} %copy.36, f32[2,256,256]{2,1,0:T(8,128)S(1)} %bitcast.433), kind=kOutput, calls=%fused_computation.321 | convolution fusion | flops 52428800 | bytes 622592 | tf_op jit(solution)/shard_map/ecij,ikj->ecik/dot_general | solution.py:112
  152.1 0.2 mul.2221
  152.3 0.2 broadcast_multiply_fusion
  152.4 0.3 fusion.274
  152.8 0.5 fusion.229
  153.3 0.5 fusion.223
  153.8 0.5 fusion.201
  154.3 0.5 fusion.200
  154.8 1.2 copy.41
  156.1 0.0 all-reduce.3.cloned.1.call-update
  156.1 1.3 fusion.239
  157.4 1.3 fusion.241
  158.8 1.6 fusion.211
  160.4 82.4 %all-reduce.3.cloned.1.call-done = f32[8,2,8192]{2,1,0:T(2,128)} async-done(((f32[8,2,8192]{2,1,0:T(2,128)}), f32[8,2,8192]{2,1,0:T(2,128)}) %all-reduce.3.cloned.1.call-update) | async-done | bytes 524304
  242.8 1.5 dynamic-slice_multiply_fusion
  244.3 0.0 copy-start
  244.4 0.2 reshape.6052
  244.5 3.5 %fusion.206 = f32[1,2,256,256]{3,1,2,0:T(2,128)S(1)} fusion(s32[256,32]{1,0:T(8,128)S(1)} %copy.36, f32[2,256,32]{2,1,0:T(8,128)S(1)} %reshape.6052), kind=kOutput, calls=%fused_computation.320 | convolution fusion | flops 52428800 | bytes 622592 | tf_op jit(solution)/shard_map/ecik,ikj->ecij/dot_general | solution.py:127
  248.0 0.5 slice_add_fusion.15
  248.4 0.4 fusion.220
  248.8 0.4 fusion.217
  249.2 0.1 subtract_bitcast_fusion.8
  249.3 1.4 fusion.213
  250.7 0.1 maximum_subtract_fusion
  250.8 0.4 fusion.236
  251.2 0.4 fusion.234
  251.6 1.4 fusion.209
  253.1 0.8 pad_maximum_fusion.6
  (21 shorter events, 0.4 us)
Async XLA Ops:
  7.2 235.6 %all-reduce.3.cloned.1.call-start = ((), (), s32[]{:S(2)}) async-start(), calls=%async_computation | async-start | bytes 1048576
  10.5 18.0 %copy-start.2 = (s32[256,32]{0,1:T(8,128)S(1)}, s32[256,32]{0,1:T(8,128)}, u32[]{:S(2)}) copy-start(s32[256,32]{0,1:T(8,128)} %param.31) | copy-start | bytes 98308
  10.5 15.6 %collective-permute-start = (f32[1,2,256,256]{3,2,1,0:T(8,128)S(1)}, f32[1,2,256,256]{3,2,1,0:T(8,128)S(1)}, u32[]{:S(2)}, u32[]{:S(2)}) collective-permute-start(f32[1,2,256,256]{3,2,1,0:T(8,128)S(1)} %get-tuple-element.149), channel_id=1, source_target_pairs={{0,8},{8,16},{16,24},{1,9},{9,17},{17,25},{2,10},{10,18},{18,26},{... | collective-permute-start | bytes 1572872 | tf_op jit(solution)/shard_map/ppermute | solution.py:18
  26.0 105.6 %copy-start.3 = (s32[256,32]{0,1:T(8,128)S(1)}, s32[256,32]{0,1:T(8,128)}, u32[]{:S(2)}) copy-start(s32[256,32]{0,1:T(8,128)} %param.30) | copy-start | bytes 98308
  26.1 105.7 %copy-start.1 = (f32[2,6,8,8]{3,2,1,0:T(8,128)S(1)}, f32[2,6,8,8]{3,2,1,0:T(8,128)}, u32[]{:S(2)}) copy-start(f32[2,6,8,8]{3,2,1,0:T(8,128)} %param.29) | copy-start | bytes 9220
  26.1 106.1 %copy-start.4 = (u32[32]{0:T(128)S(1)}, u32[32]{0:T(128)}, u32[]{:S(2)}) copy-start(u32[32]{0:T(128)} %constant.249) | copy-start | bytes 388
  26.1 73.1 %collective-permute-start.1 = (f32[1,2,256,256]{3,2,1,0:T(8,128)S(1)}, f32[1,2,256,256]{3,2,1,0:T(8,128)S(1)}, u32[]{:S(2)}, u32[]{:S(2)}) collective-permute-start(f32[1,2,256,256]{3,2,1,0:T(8,128)S(1)} %get-tuple-element.150), channel_id=1, source_target_pairs={{0,8},{8,16},{16,24},{1,9},{9,17},{17,25},{2,10},{10,18},{18,26},{... | collective-permute-start | bytes 1572872 | tf_op jit(solution)/shard_map/ppermute | solution.py:18
  129.7 15.0 %collective-permute-start.2 = (f32[1,2,256,256]{3,2,1,0:T(8,128)S(1)}, f32[1,2,256,256]{3,2,1,0:T(8,128)S(1)}, u32[]{:S(2)}, u32[]{:S(2)}) collective-permute-start(f32[1,2,256,256]{3,2,1,0:T(8,128)S(1)} %get-tuple-element.151), channel_id=1, source_target_pairs={{0,8},{8,16},{16,24},{1,9},{9,17},{17,25},{2,10},{10,18},{18,26},{... | collective-permute-start | bytes 1572872 | tf_op jit(solution)/shard_map/ppermute | solution.py:18
  244.3 9.6 %copy-start = (f32[1,2,8192]{2,1,0:T(2,128)}, f32[1,2,8192]{2,1,0:T(2,128)S(1)}, u32[]{:S(2)}) copy-start(f32[1,2,8192]{2,1,0:T(2,128)S(1)} %dynamic-slice_multiply_fusion) | copy-start | bytes 196612
Sparse Core Ops, SparseCore 0:
  156.2 86.5 all-reduce.2
where the time goes:
time: 265 us; the launch traced here: 261 us
  waiting for transfers between devices  177 us (67%)
  matrix products  27.9 us (11%)
  local copies, waits for them, and re-layouts  26.3 us (10%)
  between operations  15.7 us (6%)
  starting transfers between devices  7.43 us (3%)
  other arithmetic  6.01 us (2%)
    ppermute x3, waiting for transfers between devices, shifted_2(): return lax.ppermute(block, axis, route)  94.9 us
    unnamed x2, waiting for transfers between devices  82.4 us
    sub x1, local copies, waits for them, and re-layouts, advance(): schur_new = shifted - through  17.2 us
    ppermute x3, starting transfers between devices, shifted_2(): return lax.ppermute(block, axis, route)  7.39 us
    dot_general x5, matrix products, complex_product(): jnp.matmul(left_real + left_imag, right_real + right_imag, precision=HIGH...  6.28 us
  transfers between devices with their start and end apart: 4, of which 4 were waited for; matrix products, arithmetic and copies ran while one was open for 2% of the time, Pallas kernels for 0%

commit v1 on v0

v1 whole, which is shorter than its diff:
```python
import functools
import math

import jax
import jax.numpy as jnp
from jax import lax
from jax.experimental import pallas as pl
from jax.experimental.pallas import tpu as pltpu
from jax.sharding import PartitionSpec as P

F32 = jnp.float32
BF16 = jnp.bfloat16
MESH = pl.DeviceIdType.MESH
LANES = 128


def split(x):
    hi = x.astype(BF16)
    return hi, (x - hi.astype(F32)).astype(BF16)


def dot3(a, b, transposed=False):
    dims = (((1,), (1 if transposed else 0,)), ((), ()))
    dot = functools.partial(lax.dot_general, dimension_numbers=dims, preferred_element_type=F32)
    return dot(a[0], b[0]) + (dot(a[0], b[1]) + dot(a[1], b[0]))


def triple(re, im):
    return split(re), split(im), split(re + im)


def product(a, b):
    first, second, mixed = (dot3(x, y) for x, y in zip(a, b))
    return first - second, mixed - first - second


def take(values, index):
    return jnp.take_along_axis(values, index, axis=1, mode="promise_in_bounds")


def kernel(
    slabs, points, scale,
    en_ref, br_ref, h_ref, c_ref, k_ref, nbr_ref, mode_ref,
    green_ref, self_ref,
    hc, pg, s_ref, g_ref, rep, irep, inv_ref,
    send1, recv1, fwd1, send2, recv2, fwd2, twin_send,
):
    size = h_ref.shape[0]
    listed = nbr_ref.shape[1]
    modes = k_ref.shape[1]
    groups = LANES // listed
    packed_rows = size // groups
    chunks = size // LANES
    chips = points // 2
    me_slab, me = lax.axis_index("slab"), lax.axis_index("energy")
    par, chip = lax.rem(me, 2), lax.div(me, 2)
    twin = me + 1 - 2 * par

    barrier = pltpu.get_barrier_semaphore()

    def greet(slab, point):
        pl.semaphore_signal(barrier, inc=1, device_id=(slab, point), device_id_type=MESH)

    for d in range(1, slabs):
        greet(lax.rem(me_slab + d, slabs), me)
    greet(me_slab, twin)
    for d in range(1, chips):
        greet(me_slab, lax.rem(chip + d, chips) * 2 + par)
    pl.semaphore_wait(barrier, slabs - 1 + 1 + chips - 1)

    half_rows = size // 2

    def half(which):
        return pl.ds(pl.multiple_of(which * half_rows, half_rows), half_rows)

    def block_copy(target, item):
        return pltpu.make_async_remote_copy(
            src_ref=(h_ref, c_ref)[item].at[half(par)],
            dst_ref=hc.at[me_slab, item, half(par)],
            send_sem=send1.at[target, item],
            recv_sem=recv1.at[me_slab, item, par],
            device_id=(target, me),
            device_id_type=MESH,
        )

    def block_forward(b, item, which):
        place = hc.at[b, item, half(which)]
        return pltpu.make_async_remote_copy(
            src_ref=place, dst_ref=place,
            send_sem=fwd1.at[b, item], recv_sem=recv1.at[b, item, which],
            device_id=(me_slab, twin), device_id_type=MESH,
        )

    for target in reversed(range(1, slabs)):
        @pl.when(target > me_slab)
        def _():
            block_copy(target, 0).start()

            @pl.when(me_slab > 0)
            def _():
                block_copy(target, 1).start()

    hc[me_slab, 0] = h_ref[...]
    hc[me_slab, 1] = c_ref[...]

    row = lax.broadcasted_iota(jnp.int32, (size, size), 0)
    col = lax.broadcasted_iota(jnp.int32, (size, size), 1)
    eye = row == col

    column = lax.broadcasted_iota(jnp.int32, (size, size), 1)
    inv = jnp.full((size, size), -1, jnp.int32)
    for k in range(listed):
        inv = jnp.where(nbr_ref[:, k : k + 1] == column, k, inv)
    inv_ref[...] = inv

    group = lax.broadcasted_iota(jnp.int32, (packed_rows, LANES), 1) // listed

    def pack(ref):
        out = ref[pl.ds(0, packed_rows, stride=groups), :]
        for q in range(1, groups):
            out = jnp.where(group == q, ref[pl.ds(q, packed_rows, stride=groups), :], out)
        return out

    irep[0] = jnp.concatenate([nbr_ref[...]] * groups, axis=1)
    irep[1] = jnp.concatenate([mode_ref[...]] * groups, axis=1)

    def refine(b, through):
        s_re = jnp.where(eye, en_ref[0], 0.0) - hc[b, 0]
        s_im = jnp.where(eye, br_ref[0], 0.0)
        if through is not None:
            s_re, s_im = s_re - through[0], s_im - through[1]
        s_ref[0] = s_re
        s_ref[1] = s_im
        diag_re = jnp.where(eye, s_re, 0.0)
        diag_im = jnp.where(eye, s_im, 0.0)

        def reciprocal(axis):
            re = jnp.sum(diag_re, axis=axis, keepdims=True)
            im = jnp.sum(diag_im, axis=axis, keepdims=True)
            modulus = re * re + im * im
            return re / modulus, -im / modulus

        di_re, di_im = reciprocal(1)
        dj_re, dj_im = reciprocal(0)
        o_re = di_re * dj_re - di_im * dj_im
        o_im = di_re * dj_im + di_im * dj_re
        x_re = jnp.where(eye, 2.0 * di_re, 0.0) - (o_re * s_re - o_im * s_im)
        x_im = jnp.where(eye, 2.0 * di_im, 0.0) - (o_re * s_im + o_im * s_re)
        x = triple(x_re, x_im)
        p_re, p_im = product(triple(s_re, s_im), x)
        out_re, out_im = product(x, triple(jnp.where(eye, 2.0, 0.0) - p_re, -p_im))
        g_ref[0] = out_re
        g_ref[1] = out_im

    def arrive(b, items):
        @pl.when(b < me_slab)
        def _():
            for item in items:
                copy = block_forward(b, item, par)
                copy.wait_recv()
                copy.start()
            for item in items:
                block_forward(b, item, 1 - par).wait_recv()

    arrive(0, (0,))
    refine(0, None)

    def step(b, carry):
        arrive(b, (0, 1))
        c = split(hc[b, 1])
        through = [dot3(split(dot3(c, split(g_ref[i]))), c, transposed=True) for i in range(2)]
        refine(b, through)
        return carry

    lax.fori_loop(1, me_slab + 1, step, 0)

    for i in range(2):
        index = irep[0]
        values = take(g_ref[i, :, :LANES], index & (LANES - 1))
        for chunk in range(1, chunks):
            part = take(g_ref[i, :, chunk * LANES : (chunk + 1) * LANES], index & (LANES - 1))
            values = jnp.where(index >= chunk * LANES, part, values)
        rep[i] = values
        pg[me, i] = pack(rep.at[i])

    def pair_copy(d):
        other = lax.rem(chip + d, chips)
        return pltpu.make_async_remote_copy(
            src_ref=pg.at[me], dst_ref=pg.at[me],
            send_sem=send2.at[d], recv_sem=recv2.at[me],
            device_id=(me_slab, other * 2 + par), device_id_type=MESH,
        )

    def pair_forward(d, which):
        point = lax.rem(chip + d, chips) * 2 + which
        return pltpu.make_async_remote_copy(
            src_ref=pg.at[point], dst_ref=pg.at[point],
            send_sem=fwd2.at[d], recv_sem=recv2.at[point],
            device_id=(me_slab, twin), device_id_type=MESH,
        )

    def own_forward(point):
        return pltpu.make_async_remote_copy(
            src_ref=pg.at[point], dst_ref=pg.at[point],
            send_sem=twin_send, recv_sem=recv2.at[point],
            device_id=(me_slab, twin), device_id_type=MESH,
        )

    def each(first, last, act):
        lax.fori_loop(first, last, lambda d, carry: (act(d), carry)[1], 0)

    each(1, chips, lambda d: pair_copy(d).start())
    own_forward(me).start()

    g = triple(g_ref[0], g_ref[1])
    p_re, p_im = product(triple(s_ref[0], s_ref[1]), g)
    e_re, e_im = product(g, triple(jnp.where(eye, 2.0, 0.0) - p_re, -p_im))
    green_ref[0, 0] = e_re
    green_ref[0, 1] = e_im

    mode = pack(irep.at[1])
    nbr = pack(irep.at[0])

    def add_point(point, total):
        k_re = jnp.zeros((packed_rows, LANES), F32)
        k_im = jnp.zeros((packed_rows, LANES), F32)
        for m in range(modes):
            k_re = jnp.where(mode == m, k_ref[0, m, me, point], k_re)
            k_im = jnp.where(mode == m, k_ref[1, m, me, point], k_im)
        v_re, v_im = pg[point, 0], pg[point, 1]
        return total[0] + (k_re * v_re - k_im * v_im), total[1] + (k_re * v_im + k_im * v_re)

    zero = jnp.zeros((packed_rows, LANES), F32)
    total = add_point(me, (zero, zero))
    own_forward(twin).wait_recv()
    total = add_point(twin, total)

    def near(d, total):
        copy = pair_forward(d, par)
        copy.wait_recv()
        copy.start()
        return add_point(lax.rem(chip + d, chips) * 2 + par, total)

    def far(d, total):
        pair_forward(d, 1 - par).wait_recv()
        return add_point(lax.rem(chip + d, chips) * 2 + 1 - par, total)

    total = lax.fori_loop(1, chips, near, total)
    total = lax.fori_loop(1, chips, far, total)
    part = [scale * t for t in total]
    self_ref[0] = part[0]
    self_ref[1] = part[1]

    lane = lax.broadcasted_iota(jnp.int32, (packed_rows, LANES), 1)
    start = lane - lax.rem(lane, listed)
    summed = list(part)
    for d in range(1, listed):
        index = start + lax.rem(lane + d, listed)
        same = take(nbr, index) == nbr
        for i in range(2):
            summed[i] = summed[i] + jnp.where(same, take(part[i], index), 0.0)
    offset = lax.rem(lax.broadcasted_iota(jnp.int32, (size, LANES), 0), groups) * listed
    sigma = []
    for i in range(2):
        for q in range(groups):
            rep[i, pl.ds(q, packed_rows, stride=groups), :] = summed[i]
        values = rep[i]
        pieces = []
        for chunk in range(chunks):
            where = inv_ref[:, chunk * LANES : (chunk + 1) * LANES]
            pieces.append(
                jnp.where(where >= 0, take(values, offset + jnp.maximum(where, 0)), 0.0)
            )
        sigma.append(jnp.concatenate(pieces, axis=1))
    g = triple(g_ref[0], g_ref[1])
    p_re, p_im = product(triple(*sigma), g)
    f_re, f_im = product(g, triple(p_re, p_im))
    green_ref[0, 0] = green_ref[0, 0] + f_re
    green_ref[0, 1] = green_ref[0, 1] + f_im

    for target in range(1, slabs):
        @pl.when(target > me_slab)
        def _():
            block_copy(target, 0).wait_send()

            @pl.when(me_slab > 0)
            def _():
                block_copy(target, 1).wait_send()

    for b in range(slabs):
        @pl.when(b < me_slab)
        def _():
            for item in ((0,) if b == 0 else (0, 1)):
                block_forward(b, item, par).wait_send()

    each(1, chips, lambda d: pair_copy(d).wait_send())
    each(1, chips, lambda d: pair_forward(d, par).wait_send())
    own_forward(me).wait_send()


def body(slabs, points, energies, broadening, hamiltonian, coupling, propagator, neighbors, phonon_modes):
    assert energies.shape[0] == 1 and points % 2 == 0
    size, listed = neighbors.shape
    scale = 2.0 * math.sqrt(size / listed)
    packed = size * listed // LANES
    smem = pl.BlockSpec(memory_space=pltpu.SMEM)
    vmem = pl.BlockSpec(memory_space=pltpu.VMEM)
    dma = pltpu.SemaphoreType.DMA
    green, part = pl.pallas_call(
        functools.partial(kernel, slabs, points, scale),
        out_shape=(
            jax.ShapeDtypeStruct((1, 2, size, size), F32),
            jax.ShapeDtypeStruct((2, packed, LANES), F32),
        ),
        in_specs=[smem, smem, vmem, vmem, smem, vmem, vmem],
        out_specs=(vmem, vmem),
        scratch_shapes=[
            pltpu.VMEM((slabs, 2, size, size), F32),
            pltpu.VMEM((points, 2, packed, LANES), F32),
            pltpu.VMEM((2, size, size), F32),
            pltpu.VMEM((2, size, size), F32),
            pltpu.VMEM((2, size, LANES), F32),
            pltpu.VMEM((2, size, LANES), jnp.int32),
            pltpu.VMEM((size, size), jnp.int32),
            dma((slabs, 2)),
            dma((slabs, 2, 2)),
            dma((slabs, 2)),
            dma((points // 2,)),
            dma((points,)),
            dma((points // 2,)),
            dma,
        ],
        compiler_params=pltpu.CompilerParams(
            collective_id=0, has_side_effects=True, vmem_limit_bytes=40 * 1024 * 1024
        ),
        cost_estimate=pl.CostEstimate(
            flops=200 * size**3, bytes_accessed=8 * size * size * 4, transcendentals=0
        ),
    )(energies, broadening, hamiltonian, coupling, propagator, neighbors, phonon_modes)
    return green, part.reshape(1, 2, size * listed)


def solution(mesh):
    return jax.shard_map(
        functools.partial(body, mesh.shape["slab"], mesh.shape["energy"]),
        mesh=mesh,
        in_specs=(
            P("energy"),
            P("energy"),
            P("slab", None),
            P("slab", None),
            P(),
            P("slab", None),
            P("slab", None),
        ),
        out_specs=(P("energy", None, "slab", None), P("energy", None, "slab")),
        check_vma=False,
    )
```

time: 265 us -> 40.4 us (0.15); the launches traced: 261 us -> 40.1 us
  waiting for transfers between devices: 177 us -> 0 us
  Pallas kernels: 0 us -> 33.9 us
  matrix products: 27.9 us -> 0 us
  local copies, waits for them, and re-layouts: 26.3 us -> 4.14 us
  between operations: 15.7 us -> 2.01 us
  starting transfers between devices: 7.43 us -> 0 us
  other arithmetic: 6.01 us -> 0 us
    ppermute x3 -> x0, waiting for transfers between devices: 94.9 us -> none  [shifted_2(): return lax.ppermute(block, axis, route)]
    unnamed x2 -> x0, waiting for transfers between devices: 82.4 us -> none
    pallas_call x0 -> x1, Pallas kernels: none -> 33.9 us  [body(): pl.pallas_call(functools.partial(kernel, slabs, points, scale), out_shape...]
    dot_general x23 -> x0, matrix products: 27.9 us -> none  [the longest x5 6.28 us: complex_product(): jnp.matmul(left_real + left_imag, right_real + right_imag, precision=HIGH...]
    sub x1 -> x0, local copies, waits for them, and re-layouts: 17.2 us -> none  [advance(): schur_new = shifted - through]
    ppermute x3 -> x0, starting transfers between devices: 7.39 us -> none  [shifted_2(): return lax.ppermute(block, axis, route)]
  transfers between devices with their start and end apart: 4 -> 0, of which waited for: 4 -> 0; matrix products, arithmetic and copies ran while one was open for 2% -> 0% of each run, Pallas kernels for 0% -> 0%
where the time goes in v1:
time: 40.4 us; the launch traced here: 40.1 us
  Pallas kernels  33.9 us (84%)
  local copies, waits for them, and re-layouts  4.14 us (10%)
  between operations  2.01 us (5%)
    pallas_call x1, Pallas kernels, body(): pl.pallas_call(functools.partial(kernel, slabs, points, scale), out_shape...  33.9 us
    unnamed x9, local copies, waits for them, and re-layouts  3.47 us

profile of v1, /device:TPU:5, one launch (start us, length us, event | category | flops | bytes accessed | tf_op | source)
XLA Modules:
  0.0 40.1 jit_solution(15133466741445795305)
XLA Ops:
  0.6 0.0 copy-start
  2.0 0.9 %copy.9.nbr_ref = s32[256,32]{1,0:T(8,128)S(1)} copy(s32[256,32]{0,1:T(8,128)} %param.12) | data formatting | bytes 65536 | tf_op args[5]
  2.8 0.0 copy-start.2
  2.8 0.9 %copy.10.mode_ref = s32[256,32]{1,0:T(8,128)S(1)} copy(s32[256,32]{0,1:T(8,128)} %param.13) | data formatting | bytes 65536 | tf_op args[6]
  3.7 0.0 copy-done
  3.7 0.0 copy-done.2
  3.7 0.0 copy-start.1
  3.7 0.9 %copy-done.1 = f32[256,256]{1,0:T(8,128)S(1)} copy-done((f32[256,256]{1,0:T(8,128)S(1)}, f32[256,256]{1,0:T(8,128)}, u32[]{:S(2)}) %copy-start.1) | copy-done | bytes 262168
  4.7 33.9 %shard_map.86 = (f32[1,2,256,256]{3,2,1,0:T(8,128)S(1)}, f32[2,64,128]{2,1,0:T(8,128)S(1)}) custom-call(f32[1]{0:T(128)S(6)} %copy.12.en_ref, f32[1]{0:T(128)S(6)} %copy.13.br_ref, f32[256,256]{1,0:T(8,128)S(1)} %copy-done, f32[256,256]{1,0:T(8,128)S(1)} %copy-done.1, f32[2,6,8,8]{3,2,1,0:T(8,128)S(1)} %copy-done.2, s32[256,32]{1,0:T(8,128)S(1)} %copy.9.nbr_ref, ...), custom_call_target="tpu_custom_call" | custom-call | flops 3355443200 | bytes 2097152 | tf_op jit(solution)/shard_map/pallas_call | solution.py:309
  38.6 0.7 %reshape.7 = f32[1,2,8192]{2,1,0:T(2,128)} reshape(f32[2,64,128]{2,1,0:T(8,128)S(1)} %get-tuple-element.5) | data formatting | bytes 131072 | tf_op jit(solution)/shard_map/reshape | solution.py:340
  39.3 0.8 %copy.14 = f32[1,2,256,256]{3,2,1,0:T(8,128)} copy(f32[1,2,256,256]{3,2,1,0:T(8,128)S(1)} %get-tuple-element.8) | data formatting | bytes 1048576
Async XLA Ops:
  0.6 3.1 %copy-start = (f32[256,256]{1,0:T(8,128)S(1)}, f32[256,256]{1,0:T(8,128)}, u32[]{:S(2)}) copy-start(f32[256,256]{1,0:T(8,128)} %h_ref.1) | copy-start | bytes 786436
  2.8 0.9 %copy-start.2 = (f32[2,6,8,8]{3,2,1,0:T(8,128)S(1)}, f32[2,6,8,8]{3,2,1,0:T(8,128)}, u32[]{:S(2)}) copy-start(f32[2,6,8,8]{3,2,1,0:T(8,128)} %k_ref.1) | copy-start | bytes 9220
  3.7 1.0 %copy-start.1 = (f32[256,256]{1,0:T(8,128)S(1)}, f32[256,256]{1,0:T(8,128)}, u32[]{:S(2)}) copy-start(f32[256,256]{1,0:T(8,128)} %c_ref.1) | copy-start | bytes 786436

commit v2 on v1

--- a/solution.py
+++ b/solution.py
@@ -40,13 +40,13 @@
 
 def kernel(
     slabs, points, scale,
-    en_ref, br_ref, h_ref, c_ref, k_ref, nbr_ref, mode_ref,
+    shift_ref, h_hbm, c_hbm, k_hbm, nbr_hbm, mode_hbm,
     green_ref, self_ref,
-    hc, pg, s_ref, g_ref, rep, irep, inv_ref,
-    send1, recv1, fwd1, send2, recv2, fwd2, twin_send,
+    h_ref, hp, cb, pg, s_ref, g_ref, rep, irep, inv_ref, lists, k_ref,
+    local, send1, recv1, fwd1, send2, recv2, fwd2, twin_send,
 ):
     size = h_ref.shape[0]
-    listed = nbr_ref.shape[1]
+    listed = nbr_hbm.shape[0]
     modes = k_ref.shape[1]
     groups = LANES // listed
     packed_rows = size // groups
@@ -56,6 +56,21 @@
     par, chip = lax.rem(me, 2), lax.div(me, 2)
     twin = me + 1 - 2 * par
 
+    loads = [
+        pltpu.make_async_copy(source, target, local.at[n])
+        for n, (source, target) in enumerate(
+            (
+                (h_hbm, h_ref),
+                (nbr_hbm, lists.at[0]),
+                (mode_hbm, lists.at[1]),
+                (c_hbm, cb.at[me_slab]),
+                (k_hbm, k_ref),
+            )
+        )
+    ]
+    for load in loads:
+        load.start()
+
     barrier = pltpu.get_barrier_semaphore()
 
     def greet(slab, point):
@@ -66,17 +81,18 @@
     greet(me_slab, twin)
     for d in range(1, chips):
         greet(me_slab, lax.rem(chip + d, chips) * 2 + par)
-    pl.semaphore_wait(barrier, slabs - 1 + 1 + chips - 1)
-
     half_rows = size // 2
 
     def half(which):
         return pl.ds(pl.multiple_of(which * half_rows, half_rows), half_rows)
 
+    def place(b, item, which):
+        return hp.at[b, which] if item == 0 else cb.at[b, half(which)]
+
     def block_copy(target, item):
         return pltpu.make_async_remote_copy(
-            src_ref=(h_ref, c_ref)[item].at[half(par)],
-            dst_ref=hc.at[me_slab, item, half(par)],
+            src_ref=hp.at[me_slab, par] if item == 0 else c_hbm.at[half(par)],
+            dst_ref=place(me_slab, item, par),
             send_sem=send1.at[target, item],
             recv_sem=recv1.at[me_slab, item, par],
             device_id=(target, me),
@@ -84,33 +100,61 @@
         )
 
     def block_forward(b, item, which):
-        place = hc.at[b, item, half(which)]
         return pltpu.make_async_remote_copy(
-            src_ref=place, dst_ref=place,
+            src_ref=place(b, item, which), dst_ref=place(b, item, which),
             send_sem=fwd1.at[b, item], recv_sem=recv1.at[b, item, which],
             device_id=(me_slab, twin), device_id_type=MESH,
         )
+
+    small_row = lax.broadcasted_iota(jnp.int32, (half_rows, half_rows), 0)
+    small_col = lax.broadcasted_iota(jnp.int32, (half_rows, half_rows), 1)
+    loads[0].wait()
+    first = h_ref[:half_rows, :half_rows]
+    last = h_ref[half_rows:, half_rows:]
+    hp[me_slab, 0, :half_rows] = jnp.where(small_row <= small_col, first, last)
+    ends = jnp.sum(jnp.where(small_row == small_col, last, 0.0), axis=0, keepdims=True)
+    hp[me_slab, 0, half_rows:] = jnp.broadcast_to(ends, (8, half_rows))
+    hp[me_slab, 1, :half_rows] = h_ref[:half_rows, half_rows:]
+    hp[me_slab, 1, half_rows:] = jnp.zeros((8, half_rows), F32)
+
+    pl.semaphore_wait(barrier, slabs - 1 + 1 + chips - 1)
 
     for target in reversed(range(1, slabs)):
         @pl.when(target > me_slab)
         def _():
             block_copy(target, 0).start()
 
-            @pl.when(me_slab > 0)
-            def _():
-                block_copy(target, 1).start()
-
-    hc[me_slab, 0] = h_ref[...]
-    hc[me_slab, 1] = c_ref[...]
+    for target in reversed(range(1, slabs)):
+        @pl.when(jnp.logical_and(target > me_slab, me_slab > 0))
+        def _():
+            block_copy(target, 1).start()
+
+    def hamiltonian_block(b):
+        square = hp[b, 0, :half_rows]
+        turned = square.T
+        corner = hp[b, 1, :half_rows]
+        ends = hp[b, 0, half_rows : half_rows + 1]
+        first = jnp.where(small_row <= small_col, square, turned)
+        last = jnp.where(small_row > small_col, square, turned)
+        last = jnp.where(small_row == small_col, ends, last)
+        top = jnp.concatenate([first, corner], axis=1)
+        bottom = jnp.concatenate([corner.T, last], axis=1)
+        return jnp.concatenate([top, bottom], axis=0)
+
+    for load in loads[1:]:
+        load.wait()
 
     row = lax.broadcasted_iota(jnp.int32, (size, size), 0)
     col = lax.broadcasted_iota(jnp.int32, (size, size), 1)
     eye = row == col
 
+    irep[0] = jnp.concatenate([lists[0].T] * groups, axis=1)
+    irep[1] = jnp.concatenate([lists[1].T] * groups, axis=1)
+
     column = lax.broadcasted_iota(jnp.int32, (size, size), 1)
     inv = jnp.full((size, size), -1, jnp.int32)
     for k in range(listed):
-        inv = jnp.where(nbr_ref[:, k : k + 1] == column, k, inv)
+        inv = jnp.where(irep[0, :, k : k + 1] == column, k, inv)
     inv_ref[...] = inv
 
     group = lax.broadcasted_iota(jnp.int32, (packed_rows, LANES), 1) // listed
@@ -121,12 +165,9 @@
             out = jnp.where(group == q, ref[pl.ds(q, packed_rows, stride=groups), :], out)
         return out
 
-    irep[0] = jnp.concatenate([nbr_ref[...]] * groups, axis=1)
-    irep[1] = jnp.concatenate([mode_ref[...]] * groups, axis=1)
-
     def refine(b, through):
-        s_re = jnp.where(eye, en_ref[0], 0.0) - hc[b, 0]
-        s_im = jnp.where(eye, br_ref[0], 0.0)
+        s_re = jnp.where(eye, shift_ref[:, :1], 0.0) - hamiltonian_block(b)
+        s_im = jnp.where(eye, shift_ref[:, 1:], 0.0)
         if through is not None:
             s_re, s_im = s_re - through[0], s_im - through[1]
         s_ref[0] = s_re
@@ -167,7 +208,7 @@
 
     def step(b, carry):
         arrive(b, (0, 1))
-        c = split(hc[b, 1])
+        c = split(cb[b])
         through = [dot3(split(dot3(c, split(g_ref[i]))), c, transposed=True) for i in range(2)]
         refine(b, through)
         return carry
@@ -248,8 +289,10 @@
     total = lax.fori_loop(1, chips, near, total)
     total = lax.fori_loop(1, chips, far, total)
     part = [scale * t for t in total]
-    self_ref[0] = part[0]
-    self_ref[1] = part[1]
+    for line in range(packed_rows):
+        self_ref[0, :, line * LANES : (line + 1) * LANES] = jnp.concatenate(
+            [p[line : line + 1] for p in part], axis=0
+        )
 
     lane = lax.broadcasted_iota(jnp.int32, (packed_rows, LANES), 1)
     start = lane - lax.rem(lane, listed)
@@ -303,25 +346,30 @@
     size, listed = neighbors.shape
     scale = 2.0 * math.sqrt(size / listed)
     packed = size * listed // LANES
-    smem = pl.BlockSpec(memory_space=pltpu.SMEM)
+    hbm = pl.BlockSpec(memory_space=pltpu.HBM)
     vmem = pl.BlockSpec(memory_space=pltpu.VMEM)
     dma = pltpu.SemaphoreType.DMA
     green, part = pl.pallas_call(
         functools.partial(kernel, slabs, points, scale),
         out_shape=(
             jax.ShapeDtypeStruct((1, 2, size, size), F32),
-            jax.ShapeDtypeStruct((2, packed, LANES), F32),
+            jax.ShapeDtypeStruct((1, 2, size * listed), F32),
         ),
-        in_specs=[smem, smem, vmem, vmem, smem, vmem, vmem],
+        in_specs=[vmem] + [hbm] * 5,
         out_specs=(vmem, vmem),
         scratch_shapes=[
-            pltpu.VMEM((slabs, 2, size, size), F32),
+            pltpu.VMEM((size, size), F32),
+            pltpu.VMEM((slabs, 2, size // 2 + 8, size // 2), F32),
+            pltpu.VMEM((slabs, size, size), F32),
             pltpu.VMEM((points, 2, packed, LANES), F32),
             pltpu.VMEM((2, size, size), F32),
             pltpu.VMEM((2, size, size), F32),
             pltpu.VMEM((2, size, LANES), F32),
             pltpu.VMEM((2, size, LANES), jnp.int32),
             pltpu.VMEM((size, size), jnp.int32),
+            pltpu.VMEM((2, listed, size), jnp.int32),
+            pltpu.SMEM(propagator.shape, F32),
+            dma((5,)),
             dma((slabs, 2)),
             dma((slabs, 2, 2)),
             dma((slabs, 2)),
@@ -331,13 +379,13 @@
             dma,
         ],
         compiler_params=pltpu.CompilerParams(
-            collective_id=0, has_side_effects=True, vmem_limit_bytes=40 * 1024 * 1024
+            collective_id=0, has_side_effects=True, vmem_limit_bytes=60 * 1024 * 1024
         ),
         cost_estimate=pl.CostEstimate(
             flops=200 * size**3, bytes_accessed=8 * size * size * 4, transcendentals=0
         ),
-    )(energies, broadening, hamiltonian, coupling, propagator, neighbors, phonon_modes)
-    return green, part.reshape(1, 2, size * listed)
+    )(jnp.stack([energies, broadening], axis=1), hamiltonian, coupling, propagator, neighbors.T, phonon_modes.T)
+    return green, part
 
 
 def solution(mesh):

time: 40.4 us -> 36.8 us (0.911)
  Pallas kernels: 33.9 us -> 31.5 us
  local copies, waits for them, and re-layouts: 4.14 us -> 2.53 us
  other arithmetic: 0 us -> 0.65 us
    pallas_call x1, Pallas kernels: 33.9 us -> 31.5 us  [body(): pl.pallas_call(functools.partial(kernel, slabs, points, scale), out_shape...]
    unnamed x9 -> x4, local copies, waits for them, and re-layouts: 3.47 us -> 2.53 us
    reshape x1 -> x0, local copies, waits for them, and re-layouts: 0.67 us -> none  [body(): return (green, part.reshape(1, 2, size * listed))]
    another operation x0 -> x1, other arithmetic: none -> 0.65 us  [body(): jnp.stack([energies, broadening], axis=1)]
where the time goes in v2:
time: 36.8 us; the launch traced here: 36.6 us
  Pallas kernels  31.5 us (86%)
  local copies, waits for them, and re-layouts  2.53 us (7%)
  between operations  1.94 us (5%)
  other arithmetic  0.65 us (2%)
    pallas_call x1, Pallas kernels, body(): pl.pallas_call(functools.partial(kernel, slabs, points, scale), out_shape...  31.5 us
    unnamed x4, local copies, waits for them, and re-layouts  2.53 us

profile of v2, /device:TPU:5, one launch (start us, length us, event | category | flops | bytes accessed | tf_op | source)
XLA Modules:
  0.0 36.6 jit_solution(12218545044051661841)
XLA Ops:
  1.9 0.7 %pad_maximum_fusion.shift_ref = f32[1,2]{1,0:T(1,128)} fusion(f32[1,1]{1,0:T(1,128)} %bitcast.5, f32[1,1]{1,0:T(1,128)} %bitcast.4), kind=kLoop, calls=%fused_computation | loop fusion | flops 2 | bytes 16 | tf_op jit(solution)/shard_map/stack | solution.py:387
  2.6 31.5 %shard_map.86 = (f32[1,2,256,256]{3,2,1,0:T(8,128)}, f32[1,2,8192]{2,1,0:T(2,128)}) custom-call(f32[1,2]{1,0:T(1,128)} %pad_maximum_fusion.shift_ref, f32[256,256]{1,0:T(8,128)} %h_hbm.1, f32[256,256]{1,0:T(8,128)} %c_hbm.1, f32[2,6,8,8]{3,2,1,0:T(8,128)} %k_hbm.1, s32[32,256]{1,0:T(8,128)} %bitcast.6, s32[32,256]{1,0:T(8,128)} %bitcast.7), custom_call_target="tpu_custom_call" | custom-call | flops 3355443200 | bytes 2097152 | tf_op jit(solution)/shard_map/pallas_call | solution.py:352
  34.1 0.0 copy-start
  34.1 1.9 %copy.13 = f32[1,2,256,256]{3,2,1,0:T(8,128)} copy(f32[1,2,256,256]{3,2,1,0:T(8,128)} %get-tuple-element.4) | data formatting | bytes 1048576
  36.0 0.0 copy-done
  36.0 0.6 %copy.14 = f32[1,2,8192]{2,1,0:T(2,128)} copy(f32[1,2,8192]{2,1,0:T(2,128)S(1)} %copy-done) | data formatting | bytes 131072
Async XLA Ops:
  34.1 1.9 %copy-start = (f32[1,2,8192]{2,1,0:T(2,128)S(1)}, f32[1,2,8192]{2,1,0:T(2,128)}, u32[]{:S(2)}) copy-start(f32[1,2,8192]{2,1,0:T(2,128)} %get-tuple-element.5) | copy-start | bytes 196612

commit v3 on v2

--- a/solution.py
+++ b/solution.py
@@ -193,21 +193,34 @@
         g_ref[0] = out_re
         g_ref[1] = out_im
 
+    def pass_on(b, items):
+        copies = [block_forward(b, item, par) for item in items]
+        for copy in copies:
+            copy.wait_recv()
+            copy.start()
+
     def arrive(b, items):
+        for item in items:
+            block_forward(b, item, 1 - par).wait_recv()
+
+    @pl.when(me_slab > 0)
+    def _():
+        pass_on(0, (0,))
+        arrive(0, (0,))
+
+    refine(0, None)
+
+    def pass_on_later(b, carry):
+        pass_on(b, (0, 1))
+        return carry
+
+    lax.fori_loop(1, me_slab, pass_on_later, 0)
+
+    def step(b, carry):
         @pl.when(b < me_slab)
         def _():
-            for item in items:
-                copy = block_forward(b, item, par)
-                copy.wait_recv()
-                copy.start()
-            for item in items:
-                block_forward(b, item, 1 - par).wait_recv()
-
-    arrive(0, (0,))
-    refine(0, None)
-
-    def step(b, carry):
-        arrive(b, (0, 1))
+            arrive(b, (0, 1))
+
         c = split(cb[b])
         through = [dot3(split(dot3(c, split(g_ref[i]))), c, transposed=True) for i in range(2)]
         refine(b, through)
@@ -349,6 +362,10 @@
     hbm = pl.BlockSpec(memory_space=pltpu.HBM)
     vmem = pl.BlockSpec(memory_space=pltpu.VMEM)
     dma = pltpu.SemaphoreType.DMA
+    operands = [
+        pltpu.with_memory_space_constraint(x, pltpu.HBM)
+        for x in (hamiltonian, coupling, propagator, neighbors.T, phonon_modes.T)
+    ]
     green, part = pl.pallas_call(
         functools.partial(kernel, slabs, points, scale),
         out_shape=(
@@ -379,12 +396,12 @@
             dma,
         ],
         compiler_params=pltpu.CompilerParams(
-            collective_id=0, has_side_effects=True, vmem_limit_bytes=60 * 1024 * 1024
+            collective_id=0, has_side_effects=True, vmem_limit_bytes=40 * 1024 * 1024
         ),
         cost_estimate=pl.CostEstimate(
             flops=200 * size**3, bytes_accessed=8 * size * size * 4, transcendentals=0
         ),
-    )(jnp.stack([energies, broadening], axis=1), hamiltonian, coupling, propagator, neighbors.T, phonon_modes.T)
+    )(jnp.stack([energies, broadening], axis=1), *operands)
     return green, part
 
 

time: 36.8 us -> 33.5 us (0.910)
  Pallas kernels: 31.5 us -> 29.9 us
  local copies, waits for them, and re-layouts: 2.53 us -> 1.42 us
  other arithmetic: 0.65 us -> 0.07 us
    pallas_call x1, Pallas kernels: 31.5 us -> 29.9 us  [body(): pl.pallas_call(functools.partial(kernel, slabs, points, scale), out_shape...]
    unnamed x4 -> x2, local copies, waits for them, and re-layouts: 2.53 us -> 1.42 us
    another operation x1, other arithmetic: 0.65 us -> 0.07 us  [body(): jnp.stack([energies, broadening], axis=1)]
where the time goes in v3:
time: 33.5 us; the launch traced here: 33.4 us
  Pallas kernels  29.9 us (89%)
  between operations  1.93 us (6%)
  local copies, waits for them, and re-layouts  1.42 us (4%)
    pallas_call x1, Pallas kernels, body(): pl.pallas_call(functools.partial(kernel, slabs, points, scale), out_shape...  29.9 us
    unnamed x2, local copies, waits for them, and re-layouts  1.42 us

profile of v3, /device:TPU:5, one launch (start us, length us, event | category | flops | bytes accessed | tf_op | source)
XLA Modules:
  0.0 33.4 jit_solution(16048650400808587191)
XLA Ops:
  1.9 0.1 pad_maximum_fusion.shift_ref
  2.0 29.9 %shard_map.86 = (f32[1,2,256,256]{3,2,1,0:T(8,128)S(1)}, f32[1,2,8192]{2,1,0:T(2,128)S(1)}) custom-call(f32[1,2]{1,0:T(1,128)S(1)} %pad_maximum_fusion.shift_ref, f32[256,256]{1,0:T(8,128)} %h_hbm.1, f32[256,256]{1,0:T(8,128)} %c_hbm.1, f32[2,6,8,8]{3,2,1,0:T(8,128)} %k_hbm.1, s32[32,256]{1,0:T(8,128)} %bitcast.6, s32[32,256]{1,0:T(8,128)} %bitcast.7), custom_call_target="tpu_custom_call" | custom-call | flops 3355443200 | bytes 2097152 | tf_op jit(solution)/shard_map/pallas_call | solution.py:369
  31.9 0.8 %copy.13 = f32[1,2,256,256]{3,2,1,0:T(8,128)} copy(f32[1,2,256,256]{3,2,1,0:T(8,128)S(1)} %get-tuple-element.4) | data formatting | bytes 1048576
  32.7 0.6 %copy.14 = f32[1,2,8192]{2,1,0:T(2,128)} copy(f32[1,2,8192]{2,1,0:T(2,128)S(1)} %get-tuple-element.5) | data formatting | bytes 131072

commit v4 on v3

--- a/solution.py
+++ b/solution.py
@@ -42,7 +42,7 @@
     slabs, points, scale,
     shift_ref, h_hbm, c_hbm, k_hbm, nbr_hbm, mode_hbm,
     green_ref, self_ref,
-    h_ref, hp, cb, pg, s_ref, g_ref, rep, irep, inv_ref, lists, k_ref,
+    h_ref, hp, cb, pg, s_ref, g_ref, rep, irep, inv_ref, lists, same, total, k_ref,
     local, send1, recv1, fwd1, send2, recv2, fwd2, twin_send,
 ):
     size = h_ref.shape[0]
@@ -124,7 +124,7 @@
         def _():
             block_copy(target, 0).start()
 
-    for target in reversed(range(1, slabs)):
+    for target in range(1, slabs):
         @pl.when(jnp.logical_and(target > me_slab, me_slab > 0))
         def _():
             block_copy(target, 1).start()
@@ -237,19 +237,18 @@
         rep[i] = values
         pg[me, i] = pack(rep.at[i])
 
-    def pair_copy(d):
-        other = lax.rem(chip + d, chips)
+    def pair_copy(other):
         return pltpu.make_async_remote_copy(
             src_ref=pg.at[me], dst_ref=pg.at[me],
-            send_sem=send2.at[d], recv_sem=recv2.at[me],
+            send_sem=send2.at[other], recv_sem=recv2.at[me],
             device_id=(me_slab, other * 2 + par), device_id_type=MESH,
         )
 
-    def pair_forward(d, which):
-        point = lax.rem(chip + d, chips) * 2 + which
+    def pair_forward(other, which):
+        point = other * 2 + which
         return pltpu.make_async_remote_copy(
             src_ref=pg.at[point], dst_ref=pg.at[point],
-            send_sem=fwd2.at[d], recv_sem=recv2.at[point],
+            send_sem=fwd2.at[other], recv_sem=recv2.at[point],
             device_id=(me_slab, twin), device_id_type=MESH,
         )
 
@@ -260,10 +259,17 @@
             device_id=(me_slab, twin), device_id_type=MESH,
         )
 
-    def each(first, last, act):
-        lax.fori_loop(first, last, lambda d, carry: (act(d), carry)[1], 0)
-
-    each(1, chips, lambda d: pair_copy(d).start())
+    def partners(distances, act):
+        for distance in distances:
+            @pl.when(chip >= distance)
+            def _():
+                act(chip - distance)
+
+            @pl.when(chip + distance < chips)
+            def _():
+                act(chip + distance)
+
+    partners(reversed(range(1, chips)), lambda other: pair_copy(other).start())
     own_forward(me).start()
 
     g = triple(g_ref[0], g_ref[1])
@@ -275,46 +281,52 @@
     mode = pack(irep.at[1])
     nbr = pack(irep.at[0])
 
-    def add_point(point, total):
+    lane = lax.broadcasted_iota(jnp.int32, (packed_rows, LANES), 1)
+    start = lane - lax.rem(lane, listed)
+
+    def turned_lanes(d):
+        return start + lax.rem(lane + d, listed)
+
+    for d in range(1, listed):
+        same[d] = jnp.where(take(nbr, turned_lanes(d)) == nbr, 1.0, 0.0)
+
+    total[...] = jnp.zeros_like(total)
+
+    def add_point(point):
         k_re = jnp.zeros((packed_rows, LANES), F32)
         k_im = jnp.zeros((packed_rows, LANES), F32)
         for m in range(modes):
             k_re = jnp.where(mode == m, k_ref[0, m, me, point], k_re)
             k_im = jnp.where(mode == m, k_ref[1, m, me, point], k_im)
         v_re, v_im = pg[point, 0], pg[point, 1]
-        return total[0] + (k_re * v_re - k_im * v_im), total[1] + (k_re * v_im + k_im * v_re)
-
-    zero = jnp.zeros((packed_rows, LANES), F32)
-    total = add_point(me, (zero, zero))
-    own_forward(twin).wait_recv()
-    total = add_point(twin, total)
-
-    def near(d, total):
-        copy = pair_forward(d, par)
+        total[0] = total[0] + (k_re * v_re - k_im * v_im)
+        total[1] = total[1] + (k_re * v_im + k_im * v_re)
+
+    def near(other):
+        copy = pair_forward(other, par)
         copy.wait_recv()
         copy.start()
-        return add_point(lax.rem(chip + d, chips) * 2 + par, total)
-
-    def far(d, total):
-        pair_forward(d, 1 - par).wait_recv()
-        return add_point(lax.rem(chip + d, chips) * 2 + 1 - par, total)
-
-    total = lax.fori_loop(1, chips, near, total)
-    total = lax.fori_loop(1, chips, far, total)
-    part = [scale * t for t in total]
+        add_point(other * 2 + par)
+
+    def far(other):
+        pair_forward(other, 1 - par).wait_recv()
+        add_point(other * 2 + 1 - par)
+
+    add_point(me)
+    own_forward(twin).wait_recv()
+    add_point(twin)
+    partners(range(1, chips), near)
+    partners(range(1, chips), far)
+    part = [scale * total[i] for i in range(2)]
     for line in range(packed_rows):
         self_ref[0, :, line * LANES : (line + 1) * LANES] = jnp.concatenate(
             [p[line : line + 1] for p in part], axis=0
         )
 
-    lane = lax.broadcasted_iota(jnp.int32, (packed_rows, LANES), 1)
-    start = lane - lax.rem(lane, listed)
     summed = list(part)
     for d in range(1, listed):
-        index = start + lax.rem(lane + d, listed)
-        same = take(nbr, index) == nbr
         for i in range(2):
-            summed[i] = summed[i] + jnp.where(same, take(part[i], index), 0.0)
+            summed[i] = summed[i] + same[d] * take(part[i], turned_lanes(d))
     offset = lax.rem(lax.broadcasted_iota(jnp.int32, (size, LANES), 0), groups) * listed
     sigma = []
     for i in range(2):
@@ -349,8 +361,8 @@
             for item in ((0,) if b == 0 else (0, 1)):
                 block_forward(b, item, par).wait_send()
 
-    each(1, chips, lambda d: pair_copy(d).wait_send())
-    each(1, chips, lambda d: pair_forward(d, par).wait_send())
+    partners(range(1, chips), lambda other: pair_copy(other).wait_send())
+    partners(range(1, chips), lambda other: pair_forward(other, par).wait_send())
     own_forward(me).wait_send()
 
 
@@ -385,6 +397,8 @@
             pltpu.VMEM((2, size, LANES), jnp.int32),
             pltpu.VMEM((size, size), jnp.int32),
             pltpu.VMEM((2, listed, size), jnp.int32),
+            pltpu.VMEM((listed, packed, LANES), F32),
+            pltpu.VMEM((2, packed, LANES), F32),
             pltpu.SMEM(propagator.shape, F32),
             dma((5,)),
             dma((slabs, 2)),

time: 33.5 us -> 33.2 us (level)
  no operation moved by 1% of the time
where the time goes in v4:
time: 33.2 us; the launch traced here: 33.1 us
  Pallas kernels  29.6 us (89%)
  between operations  1.93 us (6%)
  local copies, waits for them, and re-layouts  1.42 us (4%)
    pallas_call x1, Pallas kernels, body(): pl.pallas_call(functools.partial(kernel, slabs, points, scale), out_shape...  29.6 us
    unnamed x2, local copies, waits for them, and re-layouts  1.42 us

profile of v4, /device:TPU:5, one launch (start us, length us, event | category | flops | bytes accessed | tf_op | source)
XLA Modules:
  0.0 33.1 jit_solution(8833739246446214656)
XLA Ops:
  1.9 0.1 pad_maximum_fusion.shift_ref
  2.0 29.6 %shard_map.86 = (f32[1,2,256,256]{3,2,1,0:T(8,128)S(1)}, f32[1,2,8192]{2,1,0:T(2,128)S(1)}) custom-call(f32[1,2]{1,0:T(1,128)S(1)} %pad_maximum_fusion.shift_ref, f32[256,256]{1,0:T(8,128)} %h_hbm.1, f32[256,256]{1,0:T(8,128)} %c_hbm.1, f32[2,6,8,8]{3,2,1,0:T(8,128)} %k_hbm.1, s32[32,256]{1,0:T(8,128)} %bitcast.6, s32[32,256]{1,0:T(8,128)} %bitcast.7), custom_call_target="tpu_custom_call" | custom-call | flops 3355443200 | bytes 2097152 | tf_op jit(solution)/shard_map/pallas_call | solution.py:381
  31.7 0.8 %copy.13 = f32[1,2,256,256]{3,2,1,0:T(8,128)} copy(f32[1,2,256,256]{3,2,1,0:T(8,128)S(1)} %get-tuple-element.4) | data formatting | bytes 1048576
  32.4 0.6 %copy.14 = f32[1,2,8192]{2,1,0:T(2,128)} copy(f32[1,2,8192]{2,1,0:T(2,128)S(1)} %get-tuple-element.5) | data formatting | bytes 131072

commit v5 on v4

--- a/solution.py
+++ b/solution.py
@@ -141,7 +141,7 @@
         bottom = jnp.concatenate([corner.T, last], axis=1)
         return jnp.concatenate([top, bottom], axis=0)
 
-    for load in loads[1:]:
+    for load in loads[1:3]:
         load.wait()
 
     row = lax.broadcasted_iota(jnp.int32, (size, size), 0)
@@ -215,6 +215,7 @@
         return carry
 
     lax.fori_loop(1, me_slab, pass_on_later, 0)
+    loads[3].wait()
 
     def step(b, carry):
         @pl.when(b < me_slab)
@@ -312,6 +313,7 @@
         pair_forward(other, 1 - par).wait_recv()
         add_point(other * 2 + 1 - par)
 
+    loads[4].wait()
     add_point(me)
     own_forward(twin).wait_recv()
     add_point(twin)

time: 33.2 us -> 33.2 us (level)
  no operation moved by 1% of the time
where the time goes in v5:
time: 33.2 us; the launch traced here: 33.1 us
  Pallas kernels  29.7 us (89%)
  between operations  1.93 us (6%)
  local copies, waits for them, and re-layouts  1.42 us (4%)
    pallas_call x1, Pallas kernels, body(): pl.pallas_call(functools.partial(kernel, slabs, points, scale), out_shape...  29.7 us
    unnamed x2, local copies, waits for them, and re-layouts  1.42 us

profile of v5, /device:TPU:5, one launch (start us, length us, event | category | flops | bytes accessed | tf_op | source)
XLA Modules:
  0.0 33.1 jit_solution(8874676394963158700)
XLA Ops:
  1.9 0.1 pad_maximum_fusion.shift_ref
  2.0 29.7 %shard_map.86 = (f32[1,2,256,256]{3,2,1,0:T(8,128)S(1)}, f32[1,2,8192]{2,1,0:T(2,128)S(1)}) custom-call(f32[1,2]{1,0:T(1,128)S(1)} %pad_maximum_fusion.shift_ref, f32[256,256]{1,0:T(8,128)} %h_hbm.1, f32[256,256]{1,0:T(8,128)} %c_hbm.1, f32[2,6,8,8]{3,2,1,0:T(8,128)} %k_hbm.1, s32[32,256]{1,0:T(8,128)} %bitcast.6, s32[32,256]{1,0:T(8,128)} %bitcast.7), custom_call_target="tpu_custom_call" | custom-call | flops 3355443200 | bytes 2097152 | tf_op jit(solution)/shard_map/pallas_call | solution.py:383
  31.7 0.8 %copy.13 = f32[1,2,256,256]{3,2,1,0:T(8,128)} copy(f32[1,2,256,256]{3,2,1,0:T(8,128)S(1)} %get-tuple-element.4) | data formatting | bytes 1048576
  32.5 0.6 %copy.14 = f32[1,2,8192]{2,1,0:T(2,128)} copy(f32[1,2,8192]{2,1,0:T(2,128)S(1)} %get-tuple-element.5) | data formatting | bytes 131072
